TPU v7x, 32 devices: a whole 2x2x4 slice. The times are simulated.
32 devices in a mesh: groups: 2 (over x), tx: 16 (over z, y, core).
Axes of the slice: x: 2, y: 2, z: 4, core: 2. Of those that a mesh axis runs over, the one named last changes fastest.
Arguments:
- features: bfloat16 [384, 64, 128], P(('groups', 'tx')), parts along dimension 0, may hold values from -6 to 6
- nbr_table: int32 [384, 27], P(('groups', 'tx')), parts along dimension 0, may hold values from 0 to 20, as said below
- rim_slots: int32 [32, 8], P(('groups', 'tx')), parts along dimension 0, may hold values from 0 to 12, as said below
- w_first: bfloat16 [3456, 128], P('tx'), may hold values from -0.1875 to 0.1875
- w_second: bfloat16 [3456, 128], P('tx'), may hold values from -0.1875 to 0.1875
- cotangent: bfloat16 [384, 64, 128], P(('groups', 'tx')), parts along dimension 0, may hold values from -0.059814453 to 0.059814453
Outputs:
- out_map: bfloat16 [384, 64, 128], P(('groups', 'tx')), parts along dimension 0
- grad_first: float32 [6912, 128], P(('groups', 'tx')), parts along dimension 0
- grad_second: float32 [6912, 128], P(('groups', 'tx')), parts along dimension 0
There are 2 independent parts, one for each index of `groups`. A program takes and returns all parts, laid end to end along the dimension named above; an argument that names none is the same for every part. Nothing has to cross between parts.
Inputs may be any that keep to these rules, and one draw needn't show every extreme that they name: `nbr_table`: A tile's bricks lie in 3 brick rows of 2 by 2 positions; the map strips of tiles t and t+1 touch at t's last and t+1's first brick row. Entry q of an active slot names the brick at brick offset q: a slot of the same tile (0 to 11), 12+i for entry i of the previous tile's last-row list, 12 + 4+i for entry i of the next tile's first-row list, or 20 where that brick is inactive or outside the map; every entry of an empty slot is 20. Some tiles have all 12 slots active. `rim_slots`: each half lists the active bricks of that brick row in order of position, then 12 up to 4 entries; every tile has at least one active brick in its first and in its last brick row, and some tiles have 4 in both.
All inputs are finite; a program needn't handle non-finite values.
Results may differ from a plain program's by a relative error of at most 0.0049.
Values may be sent and summed in bfloat16 or wider, within the bound.
A program may use at most 64 MiB of HBM per device.

v0:
```python
import jax
import jax.numpy as jnp
import numpy as np
from jax import lax
from jax.sharding import PartitionSpec as P

BS = 4


def padded_2(x, sides, width):
    for axis, dim in sides:
        size, length = (lax.axis_size(axis), x.shape[dim])
        up = [(i, (i + 1) % size) for i in range(size - 1)]
        down = [(j, i) for i, j in up]
        last = lax.slice_in_dim(x, length - width, length, axis=dim)
        initial = lax.slice_in_dim(x, 0, width, axis=dim)
        before = lax.ppermute(last, axis, up)
        after = lax.ppermute(initial, axis, down)
        x = jnp.concatenate([before, x, after], axis=dim)
    return x


def brick_tables(side):
    coords = np.arange(side**3)
    first = coords // (side * side)
    second = coords // side % side
    third = coords % side
    brick_code = np.zeros((side**3, 27), np.int32)
    voxel_code = np.zeros((side**3, 27), np.int32)
    for offset in range(27):
        shifts = (offset // 9 - 1, offset // 3 % 3 - 1, offset % 3 - 1)
        code = np.zeros(side**3, np.int32)
        local = np.zeros(side**3, np.int32)
        for along, step in zip((first, second, third), shifts):
            moved = along + step
            brick_step = moved // side
            code = code * 3 + brick_step + 1
            local = local * side + moved - brick_step * side
        brick_code[:, offset] = code
        voxel_code[:, offset] = local
    return (brick_code, voxel_code)


def windows(extended, table, brick_code, voxel_code):
    vox_count = extended.shape[1]
    flat = extended.reshape(-1, extended.shape[2])
    index = table[:, brick_code] * vox_count + jnp.asarray(voxel_code)[None]
    picked = jnp.take(flat, index.reshape(-1).astype(jnp.int32), axis=0)
    return picked.reshape(table.shape[0] * vox_count, -1)


def on_device(features, nbr_table, rim_slots, w_first, w_second, cotangent):
    capacity, vox_count, channels = features.shape
    rim_count = rim_slots.shape[1] // 2
    brick_code, voxel_code = brick_tables(BS)
    zero_brick = jnp.zeros((1, vox_count, channels), jnp.bfloat16)
    own_lists = rim_slots[0]

    def extend(blocks):
        padded = jnp.concatenate([blocks, zero_brick], axis=0)
        packed = jnp.take(padded, own_lists, axis=0)
        beside_all = padded_2(packed, (("tx", 0),), rim_count)
        return jnp.concatenate(
            [blocks, beside_all[:rim_count], beside_all[3 * rim_count :], zero_brick], axis=0
        )

    inputs = windows(extend(features), nbr_table, brick_code, voxel_code)
    piece = lax.all_gather(w_first, "tx", axis=0, tiled=True)
    column_block = lax.slice_in_dim(inputs, 0, piece.shape[0], axis=1)
    first_sum = jnp.dot(column_block, piece, preferred_element_type=jnp.float32)
    hidden = jax.nn.silu(first_sum).astype(jnp.bfloat16)
    second_whole = lax.all_gather(w_second, "tx", axis=0, tiled=True)
    middle = windows(
        extend(hidden.reshape(capacity, vox_count, channels)), nbr_table, brick_code, voxel_code
    )
    out_map = jnp.dot(middle, second_whole, preferred_element_type=jnp.float32).astype(jnp.bfloat16)
    out_map = out_map.reshape(capacity, vox_count, channels)
    cot_rows = cotangent.reshape(-1, channels)
    contract = (((0,), (0,)), ((), ()))
    kernel_count = second_whole.shape[0] // channels
    flipped = (
        second_whole.reshape(kernel_count, channels, channels)[::-1]
        .transpose(0, 2, 1)
        .reshape(-1, channels)
    )
    back = jnp.dot(
        windows(extend(cotangent), nbr_table, brick_code, voxel_code),
        flipped,
        preferred_element_type=jnp.float32,
    )
    sigmoid_mid = jax.nn.sigmoid(first_sum)
    grad_mid = (back * sigmoid_mid * (1.0 + first_sum * (1.0 - sigmoid_mid))).astype(jnp.bfloat16)
    term_second = lax.dot_general(middle, cot_rows, contract, preferred_element_type=jnp.float32)
    term_first = lax.dot_general(inputs, grad_mid, contract, preferred_element_type=jnp.float32)
    grad_first, grad_second = (
        lax.psum_scatter(term_first, "tx", scatter_dimension=0, tiled=True),
        lax.psum_scatter(term_second, "tx", scatter_dimension=0, tiled=True),
    )
    return (out_map, grad_first, grad_second)


def solution(mesh):
    placed = (
        P(("groups", "tx"), None, None),
        P(("groups", "tx"), None),
        P(("groups", "tx"), None),
        P("tx", None),
        P("tx", None),
        P(("groups", "tx"), None, None),
    )
    return jax.shard_map(
        on_device,
        mesh=mesh,
        in_specs=placed,
        out_specs=(
            P(("groups", "tx"), None, None),
            P(("groups", "tx"), None),
            P(("groups", "tx"), None),
        ),
        check_vma=False,
    )
```

profile of v0, /device:TPU:0, one launch (start us, length us, event | category | flops | bytes accessed | tf_op | source)
XLA Modules:
  0.0 361.7 jit_solution(17203760057079737006)
XLA Ops:
  7.2 0.7 compare_select_fusion.1
  7.9 0.7 compare_and_fusion.1
  8.6 0.9 concatenate.22
  9.5 0.9 concatenate.18
  11.7 0.7 fusion.10
  12.4 3.0 collective-permute-start
  15.4 1.3 collective-permute-start.1
  16.6 0.7 fusion.8
  17.3 5.2 %collective-permute-start.4 = (bf16[4,64,128]{2,1,0:T(8,128)(2,1)}, bf16[4,64,128]{2,1,0:T(8,128)(2,1)}, u32[]{:S(2)}, u32[]{:S(2)}) collective-permute-start(bf16[4,64,128]{2,1,0:T(8,128)(2,1)} %get-tuple-element.5), channel_id=1, source_target_pairs={{0,1},{1,2},{2,3},{3,4},{4,5},{5,6},{6,7},{7,8},{8,9},{9,10},{10,1... | collective-permute-start | bytes 196616 | tf_op jit(solution)/shard_map/ppermute | solution.py:17
  22.5 1.3 collective-permute-start.5
  23.8 0.8 copy.23
  24.6 0.7 pad_clamp_fusion.1
  25.3 3.3 gather_fusion
  30.9 27.3 %all_gather.6 = bf16[3456,128]{1,0:T(8,128)(2,1)} all-gather(bf16[216,128]{1,0:T(8,128)(2,1)S(1)} %copy-done.3), channel_id=1, replica_groups=mesh['groups'=2,'tx'=16] {'tx'}, dimensions={0}, use_global_device_ids=true | all-gather | bytes 940032 | tf_op jit(solution)/shard_map/all_gather | solution.py:68
  58.2 19.9 %all_gather.7 = bf16[3456,128]{1,0:T(8,128)(2,1)S(1)} all-gather(bf16[216,128]{1,0:T(8,128)(2,1)S(1)} %copy-done.4), channel_id=1, replica_groups=mesh['groups'=2,'tx'=16] {'tx'}, dimensions={0}, use_global_device_ids=true | all-gather | bytes 940032 | tf_op jit(solution)/shard_map/all_gather | solution.py:72
  78.2 1.3 copy.25
  79.6 1.2 maximum_maximum_fusion.2
  80.8 45.9 %gather_fusion.6 = bf16[20736,128]{1,0:T(8,128)(2,1)} fusion(bf16[1344,128]{1,0:T(8,128)(2,1)S(1)} %bitcast.30, s32[21504]{0:T(1024)} %pad_clamp_fusion), kind=kCustom, calls=%fused_computation.5.clone | custom fusion | bytes 10699776 | tf_op jit(solution)/shard_map/jit(_take)/gather | solution.py:48
  126.8 42.0 %gather_fusion.2 = bf16[20736,128]{1,0:T(8,128)(2,1)} fusion(bf16[1344,128]{1,0:T(8,128)(2,1)S(1)} %bitcast.29, s32[21504]{0:T(1024)S(1)} %copy-done.1), kind=kCustom, calls=%fused_computation.1.clone | custom fusion | bytes 10699776 | tf_op jit(solution)/shard_map/jit(_take)/gather | solution.py:48
  168.8 12.7 %broadcast_select_fusion = (bf16[20736,128]{1,0:T(8,128)(2,1)}, bf16[20736,128]{1,0:T(8,128)(2,1)}) fusion(bf16[20736,128]{1,0:T(8,128)(2,1)} %gather_fusion.6, pred[20736]{0:T(1024)(128)(4,1)S(1)} %copy-done.2, bf16[20736,128]{1,0:T(8,128)(2,1)} %gather_fusion.2), kind=kLoop, calls=%fused_computation.7 | loop fusion | flops 5308416 | bytes 21254400 | tf_op jit(solution)/shard_map/jit(_take)/select_n | solution.py:48
  181.5 10.4 %reshape.69 = bf16[768,3456]{1,0:T(8,128)(2,1)} reshape(bf16[20736,128]{1,0:T(8,128)(2,1)} %get-tuple-element.12) | data formatting | bytes 10616832 | tf_op jit(solution)/shard_map/reshape | solution.py:49
  191.9 10.4 %reshape.75 = bf16[768,3456]{1,0:T(8,128)(2,1)} reshape(bf16[20736,128]{1,0:T(8,128)(2,1)} %get-tuple-element.11) | data formatting | bytes 10616832 | tf_op jit(solution)/shard_map/reshape | solution.py:49
  202.3 4.3 %multiply_convert_fusion = (bf16[768,128]{1,0:T(8,128)(2,1)S(1)}, f32[768,128]{1,0:T(8,128)S(1)}) fusion(bf16[768,3456]{1,0:T(8,128)(2,1)} %reshape.69, bf16[3456,128]{1,0:T(8,128)(2,1)} %all_gather.6), kind=kOutput, calls=%fused_computation.20 | convolution fusion | flops 679968768 | bytes 6782976 | tf_op jit(solution)/shard_map/dot_general | solution.py:70
  207.4 2.3 collective-permute-start.2
  209.6 1.5 collective-permute-start.3
  211.1 10.7 %fusion.2 = f32[3456,128]{1,0:T(8,128)} fusion(bf16[768,3456]{1,0:T(8,128)(2,1)} %reshape.69, bf16[768,3456]{1,0:T(8,128)(2,1)} %reshape.75, bf16[3456,128]{1,0:T(8,128)(2,1)S(1)} %bitcast.33, f32[768,128]{1,0:T(8,128)S(1)} %get-tuple-element.18), kind=kOutput, calls=%fused_computation.15 | convolution fusion | flops 1359839232 | bytes 13664256 | tf_op jit(solution)/shard_map/dot_general | solution.py:94
  222.0 42.0 %gather_fusion.4 = bf16[20736,128]{1,0:T(8,128)(2,1)} fusion(bf16[1344,128]{1,0:T(8,128)(2,1)S(1)} %bitcast.31, s32[21504]{0:T(1024)S(1)} %copy-done.1), kind=kCustom, calls=%fused_computation.4.clone | custom fusion | bytes 10699776 | tf_op jit(solution)/shard_map/jit(_take)/gather | solution.py:48
  264.1 13.9 %broadcast_select_fusion.2 = bf16[20736,128]{1,0:T(8,128)(2,1)} fusion(bf16[20736,128]{1,0:T(8,128)(2,1)} %gather_fusion.4, pred[20736]{0:T(1024)(128)(4,1)S(1)} %copy-done.2), kind=kLoop, calls=%fused_computation.9 | loop fusion | flops 2654208 | bytes 10637568 | tf_op jit(solution)/shard_map/jit(_take)/select_n | solution.py:48
  278.0 10.4 %reshape.72 = bf16[768,3456]{1,0:T(8,128)(2,1)} reshape(bf16[20736,128]{1,0:T(8,128)(2,1)} %broadcast_select_fusion.2) | data formatting | bytes 10616832 | tf_op jit(solution)/shard_map/reshape | solution.py:49
  288.4 5.3 %fusion.11 = f32[3456,128]{1,0:T(8,128)} fusion(bf16[768,3456]{1,0:T(8,128)(2,1)} %reshape.72, bf16[768,128]{1,0:T(8,128)(2,1)S(1)} %bitcast.34), kind=kOutput, calls=%fused_computation.41 | convolution fusion | flops 679477248 | bytes 7274496 | tf_op jit(solution)/shard_map/dot_general | solution.py:93
  293.8 4.7 %convolution_convert_fusion = bf16[768,128]{1,0:T(8,128)(2,1)} fusion(bf16[768,3456]{1,0:T(8,128)(2,1)} %reshape.72, bf16[3456,128]{1,0:T(8,128)(2,1)S(1)} %all_gather.7), kind=kOutput, calls=%fused_computation.13 | convolution fusion | flops 679575552 | bytes 6389760 | tf_op jit(solution)/shard_map/dot_general | solution.py:76
  298.5 56.3 %reduce-scatter.9.cloned.1.call-done = f32[216,128]{1,0:T(8,128)} async-done(((f32[3456,128]{1,0:T(8,128)}), f32[216,128]{1,0:T(8,128)}) %reduce-scatter.9.cloned.1.call-update) | async-done | bytes 110608
  (42 shorter events, 4.6 us)
Async XLA Ops:
  7.2 22.1 %copy-start.5 = (s32[64,27]{1,0:T(8,128)S(1)}, s32[64,27]{1,0:T(8,128)}, u32[]{:S(2)}) copy-start(s32[64,27]{1,0:T(8,128)} %constant.22.clone) | copy-start | bytes 20740
  7.2 23.7 %copy-start.3 = (bf16[216,128]{1,0:T(8,128)(2,1)S(1)}, bf16[216,128]{1,0:T(8,128)(2,1)}, u32[]{:S(2)}) copy-start(bf16[216,128]{1,0:T(8,128)(2,1)} %param.18) | copy-start | bytes 165892
  7.2 51.0 %copy-start.4 = (bf16[216,128]{1,0:T(8,128)(2,1)S(1)}, bf16[216,128]{1,0:T(8,128)(2,1)}, u32[]{:S(2)}) copy-start(bf16[216,128]{1,0:T(8,128)(2,1)} %param.19) | copy-start | bytes 165892
  7.2 291.3 %reduce-scatter.7.cloned.1.call-start = ((), (), s32[]{:S(2)}) async-start(), calls=%async_computation.2 | async-start | bytes 1880064
  12.4 67.2 %collective-permute-start = (bf16[4,64,128]{2,1,0:T(8,128)(2,1)}, bf16[4,64,128]{2,1,0:T(8,128)(2,1)}, u32[]{:S(2)}, u32[]{:S(2)}) collective-permute-start(bf16[4,64,128]{2,1,0:T(8,128)(2,1)} %get-tuple-element.9), channel_id=1, source_target_pairs={{0,1},{1,2},{2,3},{3,4},{4,5},{5,6},{6,7},{7,8},{8,9},{9,10},{10,1... | collective-permute-start | bytes 196616 | tf_op jit(solution)/shard_map/ppermute | solution.py:17
  15.4 64.3 %collective-permute-start.1 = (bf16[4,64,128]{2,1,0:T(8,128)(2,1)}, bf16[4,64,128]{2,1,0:T(8,128)(2,1)}, u32[]{:S(2)}, u32[]{:S(2)}) collective-permute-start(bf16[4,64,128]{2,1,0:T(8,128)(2,1)} %get-tuple-element.10), channel_id=1, source_target_pairs={{1,0},{2,1},{3,2},{4,3},{5,4},{6,5},{7,6},{8,7},{9,8},{10,9},{11,1... | collective-permute-start | bytes 196616 | tf_op jit(solution)/shard_map/ppermute | solution.py:18
  17.3 62.3 %collective-permute-start.4 = (bf16[4,64,128]{2,1,0:T(8,128)(2,1)}, bf16[4,64,128]{2,1,0:T(8,128)(2,1)}, u32[]{:S(2)}, u32[]{:S(2)}) collective-permute-start(bf16[4,64,128]{2,1,0:T(8,128)(2,1)} %get-tuple-element.5), channel_id=1, source_target_pairs={{0,1},{1,2},{2,3},{3,4},{4,5},{5,6},{6,7},{7,8},{8,9},{9,10},{10,1... | collective-permute-start | bytes 196616 | tf_op jit(solution)/shard_map/ppermute | solution.py:17
  22.5 57.1 %collective-permute-start.5 = (bf16[4,64,128]{2,1,0:T(8,128)(2,1)}, bf16[4,64,128]{2,1,0:T(8,128)(2,1)}, u32[]{:S(2)}, u32[]{:S(2)}) collective-permute-start(bf16[4,64,128]{2,1,0:T(8,128)(2,1)} %get-tuple-element.6), channel_id=1, source_target_pairs={{1,0},{2,1},{3,2},{4,3},{5,4},{6,5},{7,6},{8,7},{9,8},{10,9},{11,1... | collective-permute-start | bytes 196616 | tf_op jit(solution)/shard_map/ppermute | solution.py:18
  28.5 51.1 %copy-start = (bf16[12,64,128]{2,1,0:T(8,128)(2,1)S(1)}, bf16[12,64,128]{2,1,0:T(8,128)(2,1)}, u32[]{:S(2)}) copy-start(bf16[12,64,128]{2,1,0:T(8,128)(2,1)} %param.20) | copy-start | bytes 589828
  80.8 46.0 %copy-start.1 = (s32[21504]{0:T(1024)S(1)}, s32[21504]{0:T(1024)}, u32[]{:S(2)}) copy-start(s32[21504]{0:T(1024)} %pad_clamp_fusion) | copy-start | bytes 258052
  126.8 42.1 %copy-start.2 = (pred[20736]{0:T(1024)(128)(4,1)S(1)}, pred[20736]{0:T(1024)(128)(4,1)}, u32[]{:S(2)}) copy-start(pred[20736]{0:T(1024)(128)(4,1)} %compare_and_fusion) | copy-start | bytes 62212
  207.4 14.6 %collective-permute-start.2 = (bf16[4,64,128]{2,1,0:T(8,128)(2,1)S(1)}, bf16[4,64,128]{2,1,0:T(8,128)(2,1)S(1)}, u32[]{:S(2)}, u32[]{:S(2)}) collective-permute-start(bf16[4,64,128]{2,1,0:T(8,128)(2,1)S(1)} %get-tuple-element.7), channel_id=1, source_target_pairs={{0,1},{1,2},{2,3},{3,4},{4,5},{5,6},{6,7},{7,8},{8,9},{9,10},{10,1... | collective-permute-start | bytes 196616 | tf_op jit(solution)/shard_map/ppermute | solution.py:17
  209.6 12.3 %collective-permute-start.3 = (bf16[4,64,128]{2,1,0:T(8,128)(2,1)S(1)}, bf16[4,64,128]{2,1,0:T(8,128)(2,1)S(1)}, u32[]{:S(2)}, u32[]{:S(2)}) collective-permute-start(bf16[4,64,128]{2,1,0:T(8,128)(2,1)S(1)} %get-tuple-element.8), channel_id=1, source_target_pairs={{1,0},{2,1},{3,2},{4,3},{5,4},{6,5},{7,6},{8,7},{9,8},{10,9},{11,1... | collective-permute-start | bytes 196616 | tf_op jit(solution)/shard_map/ppermute | solution.py:18
  221.9 132.9 %reduce-scatter.9.cloned.1.call-start = ((), (), s32[]{:S(2)}) async-start(), calls=%async_computation.3 | async-start | bytes 1880064
Sparse Core Ops, SparseCore 0:
  222.0 60.9 reduce-scatter.6
  293.9 60.8 reduce-scatter.8
where the time goes:
time: 365 us; the launch traced here: 362 us
  local copies, waits for them, and re-layouts  173 us (47%)
  waiting for transfers between devices  56.4 us (15%)
  blocking collectives  47.2 us (13%)
  other arithmetic  31.4 us (9%)
  matrix products  25.1 us (7%)
  starting transfers between devices  14.5 us (4%)
  between operations  14.3 us (4%)
    gather x3, local copies, waits for them, and re-layouts, windows(): picked = jnp.take(flat, index.reshape(-1).astype(jnp.int32), axis=0)  130 us
    unnamed x4, waiting for transfers between devices  56.4 us
    reshape x3, local copies, waits for them, and re-layouts, windows(): return picked.reshape(table.shape[0] * vox_count, -1)  31.3 us
    all_gather x1, blocking collectives, on_device(): piece = lax.all_gather(w_first, 'tx', axis=0, tiled=True)  27.3 us
    select_n x3, other arithmetic, windows(): picked = jnp.take(flat, index.reshape(-1).astype(jnp.int32), axis=0)  26.5 us
    all_gather x1, blocking collectives, on_device(): second_whole = lax.all_gather(w_second, 'tx', axis=0, tiled=True)  19.9 us
    dot_general x1, matrix products, on_device(): lax.dot_general(inputs, grad_mid, contract, preferred_element_type=jnp.fl...  10.7 us
    ppermute x3, starting transfers between devices, padded_2(): before = lax.ppermute(last, axis, up)  10.4 us
  transfers between devices with their start and end apart: 8, of which 1 were waited for; matrix products, arithmetic and copies ran while one was open for 27% of the time, Pallas kernels for 0%

commit v1 on v0

--- a/solution.py
+++ b/solution.py
@@ -5,6 +5,24 @@
 from jax.sharding import PartitionSpec as P
 
 BS = 4
+
+
+def laid_out(blocks, dim):
+    blocks = jnp.moveaxis(blocks, 0, dim)
+    lengths = blocks.shape
+    return blocks.reshape(*lengths[:dim], lengths[dim] * lengths[dim + 1], *lengths[dim + 2 :])
+
+
+def grow_blocks(x, axis):
+    devices = lax.axis_size(axis)
+    pieces = x[None]
+    for level in range(devices.bit_length() - 1):
+        bit = 1 << level
+        other = lax.ppermute(pieces, axis, [(i, i ^ bit) for i in range(devices)])
+        both = jnp.stack([pieces, other])
+        upper = lax.axis_index(axis) >> level & 1
+        pieces = jnp.where(upper == 0, both, both[::-1]).reshape(-1, *x.shape)
+    return pieces
 
 
 def padded_2(x, sides, width):
@@ -65,7 +83,7 @@
         )
 
     inputs = windows(extend(features), nbr_table, brick_code, voxel_code)
-    piece = lax.all_gather(w_first, "tx", axis=0, tiled=True)
+    piece = laid_out(grow_blocks(w_first, "tx"), 0)
     column_block = lax.slice_in_dim(inputs, 0, piece.shape[0], axis=1)
     first_sum = jnp.dot(column_block, piece, preferred_element_type=jnp.float32)
     hidden = jax.nn.silu(first_sum).astype(jnp.bfloat16)

time: 365 us -> 353 us (0.967)
  blocking collectives: 47.2 us -> 24.3 us
  waiting for transfers between devices: 56.4 us -> 64.1 us
    all_gather x1 -> x0, blocking collectives: 27.3 us -> none  [on_device(): piece = lax.all_gather(w_first, 'tx', axis=0, tiled=True)]
    all_gather x1, blocking collectives: 19.9 us -> 24.3 us  [on_device(): second_whole = lax.all_gather(w_second, 'tx', axis=0, tiled=True)]
    unnamed x4, waiting for transfers between devices: 56.4 us -> 60.3 us
    ppermute x0 -> x4, waiting for transfers between devices: none -> 3.82 us  [grow_blocks(): other = lax.ppermute(pieces, axis, [(i, i ^ bit) for i in range(devices)])]
  transfers between devices with their start and end apart: 8 -> 12, of which waited for: 1 -> 2; matrix products, arithmetic and copies ran while one was open for 27% -> 63% of each run, Pallas kernels for 0% -> 0%
where the time goes in v1:
time: 353 us; the launch traced here: 350 us
  local copies, waits for them, and re-layouts  174 us (49%)
  waiting for transfers between devices  64.1 us (18%)
  other arithmetic  32.9 us (9%)
  matrix products  24.8 us (7%)
  blocking collectives  24.3 us (7%)
  starting transfers between devices  15.9 us (5%)
  between operations  14.4 us (4%)
    gather x3, local copies, waits for them, and re-layouts, windows(): picked = jnp.take(flat, index.reshape(-1).astype(jnp.int32), axis=0)  130 us
    unnamed x4, waiting for transfers between devices  60.3 us
    reshape x3, local copies, waits for them, and re-layouts, windows(): return picked.reshape(table.shape[0] * vox_count, -1)  31.3 us
    select_n x3, other arithmetic, windows(): picked = jnp.take(flat, index.reshape(-1).astype(jnp.int32), axis=0)  26.6 us
    all_gather x1, blocking collectives, on_device(): second_whole = lax.all_gather(w_second, 'tx', axis=0, tiled=True)  24.3 us
    dot_general x1, matrix products, on_device(): lax.dot_general(inputs, grad_mid, contract, preferred_element_type=jnp.fl...  10.8 us
    ppermute x3, starting transfers between devices, padded_2(): before = lax.ppermute(last, axis, up)  9.43 us
  transfers between devices with their start and end apart: 12, of which 2 were waited for; matrix products, arithmetic and copies ran while one was open for 63% of the time, Pallas kernels for 0%

profile of v1, /device:TPU:0, one launch (start us, length us, event | category | flops | bytes accessed | tf_op | source)
XLA Modules:
  0.0 350.0 jit_solution(15262538560965138177)
XLA Ops:
  8.6 0.9 concatenate.22
  9.5 0.9 concatenate.18
  11.7 0.7 fusion.12
  12.4 3.0 collective-permute-start
  15.4 1.3 collective-permute-start.1
  17.3 5.2 %collective-permute-start.8 = (bf16[4,64,128]{2,1,0:T(8,128)(2,1)}, bf16[4,64,128]{2,1,0:T(8,128)(2,1)}, u32[]{:S(2)}, u32[]{:S(2)}) collective-permute-start(bf16[4,64,128]{2,1,0:T(8,128)(2,1)} %get-tuple-element.5), channel_id=1, source_target_pairs={{0,1},{1,2},{2,3},{3,4},{4,5},{5,6},{6,7},{7,8},{8,9},{9,10},{10,1... | collective-permute-start | bytes 196616 | tf_op jit(solution)/shard_map/ppermute | solution.py:35
  22.5 1.3 collective-permute-start.9
  23.8 1.8 collective-permute-start.2
  25.6 0.8 copy.23
  26.4 0.7 pad_clamp_fusion.1
  27.1 3.3 gather_fusion
  32.1 24.3 %all_gather.3 = bf16[3456,128]{1,0:T(8,128)(2,1)S(1)} all-gather(bf16[216,128]{1,0:T(8,128)(2,1)S(1)} %copy-done.5), channel_id=1, replica_groups=mesh['groups'=2,'tx'=16] {'tx'}, dimensions={0}, use_global_device_ids=true | all-gather | bytes 940032 | tf_op jit(solution)/shard_map/all_gather | solution.py:90
  57.2 1.3 copy.25
  58.6 3.8 %collective-permute-done.3 = bf16[2,216,128]{2,1,0:T(8,128)(2,1)S(1)} collective-permute-done((bf16[2,216,128]{2,1,0:T(8,128)(2,1)S(1)}, bf16[2,216,128]{2,1,0:T(8,128)(2,1)S(1)}, u32[]{:S(2)}, u32[]{:S(2)}) %collective-permute-start.3) | collective-permute-done | bytes 110624 | tf_op jit(solution)/shard_map/ppermute | solution.py:21
  62.7 1.2 maximum_maximum_fusion.2
  63.9 46.0 %gather_fusion.6 = bf16[20736,128]{1,0:T(8,128)(2,1)} fusion(bf16[1344,128]{1,0:T(8,128)(2,1)S(1)} %bitcast.45, s32[21504]{0:T(1024)} %pad_clamp_fusion), kind=kCustom, calls=%fused_computation.5.clone | custom fusion | bytes 10699776 | tf_op jit(solution)/shard_map/jit(_take)/gather | solution.py:66
  109.8 42.1 %gather_fusion.2 = bf16[20736,128]{1,0:T(8,128)(2,1)} fusion(bf16[1344,128]{1,0:T(8,128)(2,1)S(1)} %bitcast.44, s32[21504]{0:T(1024)S(1)} %copy-done.1), kind=kCustom, calls=%fused_computation.1.clone | custom fusion | bytes 10699776 | tf_op jit(solution)/shard_map/jit(_take)/gather | solution.py:66
  151.9 0.7 copy-done.2
  152.6 1.0 pad_maximum_fusion.1
  154.1 12.7 %broadcast_select_fusion = (bf16[20736,128]{1,0:T(8,128)(2,1)}, bf16[20736,128]{1,0:T(8,128)(2,1)}) fusion(bf16[20736,128]{1,0:T(8,128)(2,1)} %gather_fusion.6, pred[20736]{0:T(1024)(128)(4,1)S(1)} %copy-done.3, bf16[20736,128]{1,0:T(8,128)(2,1)} %gather_fusion.2), kind=kLoop, calls=%fused_computation.7 | loop fusion | flops 5308416 | bytes 21254400 | tf_op jit(solution)/shard_map/jit(_take)/select_n | solution.py:66
  166.8 10.4 %reshape.78 = bf16[768,3456]{1,0:T(8,128)(2,1)} reshape(bf16[20736,128]{1,0:T(8,128)(2,1)} %get-tuple-element.14) | data formatting | bytes 10616832 | tf_op jit(solution)/shard_map/reshape | solution.py:67
  177.2 10.5 %reshape.87 = bf16[768,3456]{1,0:T(8,128)(2,1)} reshape(bf16[20736,128]{1,0:T(8,128)(2,1)} %get-tuple-element.13) | data formatting | bytes 10616832 | tf_op jit(solution)/shard_map/reshape | solution.py:67
  188.0 4.1 %multiply_convert_fusion = (bf16[768,128]{1,0:T(8,128)(2,1)S(1)}, f32[768,128]{1,0:T(8,128)S(1)}) fusion(bf16[768,3456]{1,0:T(8,128)(2,1)} %reshape.78, bf16[3456,128]{1,0:T(8,128)(2,1)S(1)} %bitcast.54), kind=kOutput, calls=%fused_computation.24 | convolution fusion | flops 679968768 | bytes 6782976 | tf_op jit(solution)/shard_map/dot_general | solution.py:88
  192.7 1.3 collective-permute-start.6
  194.0 1.5 collective-permute-start.7
  195.5 10.8 %fusion.2 = f32[3456,128]{1,0:T(8,128)} fusion(bf16[768,3456]{1,0:T(8,128)(2,1)} %reshape.78, bf16[768,3456]{1,0:T(8,128)(2,1)} %reshape.87, bf16[3456,128]{1,0:T(8,128)(2,1)S(1)} %bitcast.48, f32[768,128]{1,0:T(8,128)S(1)} %get-tuple-element.20), kind=kOutput, calls=%fused_computation.17 | convolution fusion | flops 1359839232 | bytes 13664256 | tf_op jit(solution)/shard_map/dot_general | solution.py:112
  206.5 42.1 %gather_fusion.4 = bf16[20736,128]{1,0:T(8,128)(2,1)} fusion(bf16[1344,128]{1,0:T(8,128)(2,1)S(1)} %bitcast.46, s32[21504]{0:T(1024)S(1)} %copy-done.1), kind=kCustom, calls=%fused_computation.4.clone | custom fusion | bytes 10699776 | tf_op jit(solution)/shard_map/jit(_take)/gather | solution.py:66
  248.6 13.9 %broadcast_select_fusion.2 = bf16[20736,128]{1,0:T(8,128)(2,1)} fusion(bf16[20736,128]{1,0:T(8,128)(2,1)} %gather_fusion.4, pred[20736]{0:T(1024)(128)(4,1)S(1)} %copy-done.3), kind=kLoop, calls=%fused_computation.9 | loop fusion | flops 2654208 | bytes 10637568 | tf_op jit(solution)/shard_map/jit(_take)/select_n | solution.py:66
  262.5 10.4 %reshape.84 = bf16[768,3456]{1,0:T(8,128)(2,1)} reshape(bf16[20736,128]{1,0:T(8,128)(2,1)} %broadcast_select_fusion.2) | data formatting | bytes 10616832 | tf_op jit(solution)/shard_map/reshape | solution.py:67
  272.9 5.3 %fusion.13 = f32[3456,128]{1,0:T(8,128)} fusion(bf16[768,3456]{1,0:T(8,128)(2,1)} %reshape.84, bf16[768,128]{1,0:T(8,128)(2,1)S(1)} %bitcast.51), kind=kOutput, calls=%fused_computation.51 | convolution fusion | flops 679477248 | bytes 7274496 | tf_op jit(solution)/shard_map/dot_general | solution.py:111
  278.2 4.7 %convolution_convert_fusion = bf16[768,128]{1,0:T(8,128)(2,1)} fusion(bf16[768,3456]{1,0:T(8,128)(2,1)} %reshape.84, bf16[3456,128]{1,0:T(8,128)(2,1)S(1)} %all_gather.3), kind=kOutput, calls=%fused_computation.14 | convolution fusion | flops 679575552 | bytes 6389760 | tf_op jit(solution)/shard_map/dot_general | solution.py:94
  282.9 60.2 %reduce-scatter.9.cloned.1.call-done = f32[216,128]{1,0:T(8,128)} async-done(((f32[3456,128]{1,0:T(8,128)}), f32[216,128]{1,0:T(8,128)}) %reduce-scatter.9.cloned.1.call-update) | async-done | bytes 110608
  (59 shorter events, 7.7 us)
Async XLA Ops:
  7.2 23.9 %copy-start.6 = (s32[64,27]{1,0:T(8,128)S(1)}, s32[64,27]{1,0:T(8,128)}, u32[]{:S(2)}) copy-start(s32[64,27]{1,0:T(8,128)} %constant.26.clone) | copy-start | bytes 20740
  7.2 49.8 %copy-start.4 = (bf16[216,128]{1,0:T(8,128)(2,1)S(1)}, bf16[216,128]{1,0:T(8,128)(2,1)}, u32[]{:S(2)}) copy-start(bf16[216,128]{1,0:T(8,128)(2,1)} %param.18) | copy-start | bytes 165892
  7.2 24.9 %copy-start.5 = (bf16[216,128]{1,0:T(8,128)(2,1)S(1)}, bf16[216,128]{1,0:T(8,128)(2,1)}, u32[]{:S(2)}) copy-start(bf16[216,128]{1,0:T(8,128)(2,1)} %param.19) | copy-start | bytes 165892
  7.2 275.7 %reduce-scatter.7.cloned.1.call-start = ((), (), s32[]{:S(2)}) async-start(), calls=%async_computation.2 | async-start | bytes 1880064
  12.4 50.2 %collective-permute-start = (bf16[4,64,128]{2,1,0:T(8,128)(2,1)}, bf16[4,64,128]{2,1,0:T(8,128)(2,1)}, u32[]{:S(2)}, u32[]{:S(2)}) collective-permute-start(bf16[4,64,128]{2,1,0:T(8,128)(2,1)} %get-tuple-element.9), channel_id=1, source_target_pairs={{0,1},{1,2},{2,3},{3,4},{4,5},{5,6},{6,7},{7,8},{8,9},{9,10},{10,1... | collective-permute-start | bytes 196616 | tf_op jit(solution)/shard_map/ppermute | solution.py:35
  15.4 47.3 %collective-permute-start.1 = (bf16[4,64,128]{2,1,0:T(8,128)(2,1)}, bf16[4,64,128]{2,1,0:T(8,128)(2,1)}, u32[]{:S(2)}, u32[]{:S(2)}) collective-permute-start(bf16[4,64,128]{2,1,0:T(8,128)(2,1)} %get-tuple-element.10), channel_id=1, source_target_pairs={{1,0},{2,1},{3,2},{4,3},{5,4},{6,5},{7,6},{8,7},{9,8},{10,9},{11,1... | collective-permute-start | bytes 196616 | tf_op jit(solution)/shard_map/ppermute | solution.py:36
  17.3 45.3 %collective-permute-start.8 = (bf16[4,64,128]{2,1,0:T(8,128)(2,1)}, bf16[4,64,128]{2,1,0:T(8,128)(2,1)}, u32[]{:S(2)}, u32[]{:S(2)}) collective-permute-start(bf16[4,64,128]{2,1,0:T(8,128)(2,1)} %get-tuple-element.5), channel_id=1, source_target_pairs={{0,1},{1,2},{2,3},{3,4},{4,5},{5,6},{6,7},{7,8},{8,9},{9,10},{10,1... | collective-permute-start | bytes 196616 | tf_op jit(solution)/shard_map/ppermute | solution.py:35
  22.5 40.2 %collective-permute-start.9 = (bf16[4,64,128]{2,1,0:T(8,128)(2,1)}, bf16[4,64,128]{2,1,0:T(8,128)(2,1)}, u32[]{:S(2)}, u32[]{:S(2)}) collective-permute-start(bf16[4,64,128]{2,1,0:T(8,128)(2,1)} %get-tuple-element.6), channel_id=1, source_target_pairs={{1,0},{2,1},{3,2},{4,3},{5,4},{6,5},{7,6},{8,7},{9,8},{10,9},{11,1... | collective-permute-start | bytes 196616 | tf_op jit(solution)/shard_map/ppermute | solution.py:36
  23.8 33.2 %collective-permute-start.2 = (bf16[1,216,128]{2,1,0:T(8,128)(2,1)}, bf16[1,216,128]{2,1,0:T(8,128)(2,1)S(1)}, u32[]{:S(2)}, u32[]{:S(2)}) collective-permute-start(bf16[1,216,128]{2,1,0:T(8,128)(2,1)} %bitcast.60), channel_id=1, source_target_pairs={{0,1},{1,0},{2,3},{3,2},{4,5},{5,4},{6,7},{7,6},{8,9},{9,8},{10,11... | collective-permute-start | bytes 165896 | tf_op jit(solution)/shard_map/ppermute | solution.py:21
  30.4 32.3 %copy-start = (bf16[12,64,128]{2,1,0:T(8,128)(2,1)S(1)}, bf16[12,64,128]{2,1,0:T(8,128)(2,1)}, u32[]{:S(2)}) copy-start(bf16[12,64,128]{2,1,0:T(8,128)(2,1)} %param.20) | copy-start | bytes 589828
  57.1 5.4 %collective-permute-start.3 = (bf16[2,216,128]{2,1,0:T(8,128)(2,1)S(1)}, bf16[2,216,128]{2,1,0:T(8,128)(2,1)S(1)}, u32[]{:S(2)}, u32[]{:S(2)}) collective-permute-start(bf16[2,216,128]{2,1,0:T(8,128)(2,1)S(1)} %get-tuple-element.12), channel_id=1, source_target_pairs={{0,2},{1,3},{2,0},{3,1},{4,6},{5,7},{6,4},{7,5},{8,10},{9,11},{10,... | collective-permute-start | bytes 331784 | tf_op jit(solution)/shard_map/ppermute | solution.py:21
  62.5 89.4 %collective-permute-start.4 = (bf16[4,216,128]{2,1,0:T(8,128)(2,1)S(1)}, bf16[4,216,128]{2,1,0:T(8,128)(2,1)S(1)}, u32[]{:S(2)}, u32[]{:S(2)}) collective-permute-start(bf16[4,216,128]{2,1,0:T(8,128)(2,1)S(1)} %bitcast.52), channel_id=1, source_target_pairs={{0,4},{1,5},{2,6},{3,7},{4,0},{5,1},{6,2},{7,3},{8,12},{9,13},{10,... | collective-permute-start | bytes 663560 | tf_op jit(solution)/shard_map/ppermute | solution.py:21
  63.9 46.0 %copy-start.1 = (s32[21504]{0:T(1024)S(1)}, s32[21504]{0:T(1024)}, u32[]{:S(2)}) copy-start(s32[21504]{0:T(1024)} %pad_clamp_fusion) | copy-start | bytes 258052
  109.8 44.3 %copy-start.3 = (pred[20736]{0:T(1024)(128)(4,1)S(1)}, pred[20736]{0:T(1024)(128)(4,1)}, u32[]{:S(2)}) copy-start(pred[20736]{0:T(1024)(128)(4,1)} %compare_and_fusion) | copy-start | bytes 62212
  151.9 0.7 copy-start.2
  153.7 34.0 %collective-permute-start.5 = (bf16[8,216,128]{2,1,0:T(8,128)(2,1)S(1)}, bf16[8,216,128]{2,1,0:T(8,128)(2,1)S(1)}, u32[]{:S(2)}, u32[]{:S(2)}) collective-permute-start(bf16[8,216,128]{2,1,0:T(8,128)(2,1)S(1)} %bitcast.49), channel_id=1, source_target_pairs={{0,8},{1,9},{2,10},{3,11},{4,12},{5,13},{6,14},{7,15},{8,0},{9,1},... | collective-permute-start | bytes 1327112 | tf_op jit(solution)/shard_map/ppermute | solution.py:21
  192.7 13.6 %collective-permute-start.6 = (bf16[4,64,128]{2,1,0:T(8,128)(2,1)S(1)}, bf16[4,64,128]{2,1,0:T(8,128)(2,1)S(1)}, u32[]{:S(2)}, u32[]{:S(2)}) collective-permute-start(bf16[4,64,128]{2,1,0:T(8,128)(2,1)S(1)} %get-tuple-element.7), channel_id=1, source_target_pairs={{0,1},{1,2},{2,3},{3,4},{4,5},{5,6},{6,7},{7,8},{8,9},{9,10},{10,1... | collective-permute-start | bytes 196616 | tf_op jit(solution)/shard_map/ppermute | solution.py:35
  194.0 12.3 %collective-permute-start.7 = (bf16[4,64,128]{2,1,0:T(8,128)(2,1)S(1)}, bf16[4,64,128]{2,1,0:T(8,128)(2,1)S(1)}, u32[]{:S(2)}, u32[]{:S(2)}) collective-permute-start(bf16[4,64,128]{2,1,0:T(8,128)(2,1)S(1)} %get-tuple-element.8), channel_id=1, source_target_pairs={{1,0},{2,1},{3,2},{4,3},{5,4},{6,5},{7,6},{8,7},{9,8},{10,9},{11,1... | collective-permute-start | bytes 196616 | tf_op jit(solution)/shard_map/ppermute | solution.py:36
  206.3 136.9 %reduce-scatter.9.cloned.1.call-start = ((), (), s32[]{:S(2)}) async-start(), calls=%async_computation.3 | async-start | bytes 1880064
Sparse Core Ops, SparseCore 0:
  206.4 64.7 reduce-scatter.6
  278.3 64.7 reduce-scatter.8
